TPU v7x, 32 devices: a whole 2x2x4 slice. The times are simulated.
32 devices in a mesh: dp: 2 (over core), seq: 16 (over z, y, x).
Axes of the slice: x: 2, y: 2, z: 4, core: 2. Of those that a mesh axis runs over, the one named last changes fastest.
Arguments:
- mapped_askers: bfloat16 [2, 4096, 1024], P('dp', 'seq'), may hold values from -6 to 6
- mapped_lookups: bfloat16 [2, 4096, 1024], P('dp', 'seq'), may hold values from -6 to 6
- mapped_contents: bfloat16 [2, 4096, 1024], P('dp', 'seq'), may hold values from -24 to 24
- result_cotangent: bfloat16 [2, 4096, 1024], P('dp', 'seq'), may hold values from -6 to 6
- result_weight_matrix: bfloat16 [1024, 1024], replicated, may hold values from -0.1875 to 0.1875
- reference_comb_shift: int32 [16, 32], P('seq'), may hold values from 0 to 7
- symbol_frame_label: int32 [4096], replicated, may hold values from 0 to 7, never falling along the last dimension, each value on 1 to 1024 neighbouring positions
Outputs:
- sublayer_out: bfloat16 [2, 4096, 1024], P('dp', 'seq')
- query_grad: bfloat16 [2, 4096, 1024], P('dp', 'seq')
- key_grad: bfloat16 [2, 4096, 1024], P('dp', 'seq')
- value_grad: bfloat16 [2, 4096, 1024], P('dp', 'seq')
- weight_grad: float32 [1024, 1024], P(('dp', 'seq'))
All inputs are finite; a program needn't handle non-finite values.
Results may differ from a plain program's by a relative error of at most 0.012.
Values may be sent and summed in bfloat16 or wider, within the bound.
A program may use at most 128 MiB of HBM per device.

v0:
```python
import math

import jax
import jax.numpy as jnp
from jax import lax
from jax.sharding import PartitionSpec as P

HEADS = 8
HALF_SPAN = 256
FRAME_SHARDS = 8


def with_halo(value, sides, width):
    for axis, dim in sides:
        peers, length = (lax.axis_size(axis), value.shape[dim])
        up = [(i, (i + 1) % peers) for i in range(peers - 1)]
        down = [(j, i) for i, j in up]
        last = lax.slice_in_dim(value, length - width, length, axis=dim)
        initial = lax.slice_in_dim(value, 0, width, axis=dim)
        before = lax.ppermute(last, axis, up)
        after = lax.ppermute(initial, axis, down)
        value = jnp.concatenate([before, value, after], axis=dim)
    return value


def swapped(value, axis, apart):
    return lax.ppermute(value, axis, [(i, i ^ 1 << apart) for i in range(lax.axis_size(axis))])


def joint_admit_filter(neighbor_frame_label, overall_line_number):
    query_rows = jnp.arange(overall_line_number)[:, None] + HALF_SPAN
    key_cols = jnp.arange(overall_line_number + 2 * HALF_SPAN)[None, :]
    inside_local_distance = jnp.abs(query_rows - key_cols) <= HALF_SPAN
    asker_frame_label = neighbor_frame_label[HALF_SPAN : HALF_SPAN + overall_line_number]
    same_frame_filter = asker_frame_label[:, None] == neighbor_frame_label[None, :]
    return inside_local_distance & same_frame_filter


def attend_shard(query_block, key_win, val_win, key_pil, val_pil, local_admit_filter, grad_att):
    head_dim = query_block.shape[1] // HEADS
    scaling = 1.0 / math.sqrt(head_dim)

    def split_heads(matrix):
        return jnp.transpose(matrix.reshape(matrix.shape[0], HEADS, head_dim), (1, 0, 2))

    def join_heads(matrix):
        return jnp.transpose(matrix, (1, 0, 2)).reshape(matrix.shape[1], HEADS * head_dim)

    def one_head(round_arguments):
        query_head, key_head, val_head, pilot_key, pilot_val, grad_head = round_arguments
        score_win = jnp.dot(query_head, key_head.T, preferred_element_type=jnp.float32) * scaling
        score_win = jnp.where(local_admit_filter, score_win, -jnp.inf)
        score_pil = jnp.dot(query_head, pilot_key.T, preferred_element_type=jnp.float32) * scaling
        row_max = jnp.maximum(jnp.max(score_win, axis=1), jnp.max(score_pil, axis=1))[:, None]
        exp_win = jnp.exp(score_win - row_max)
        exp_pil = jnp.exp(score_pil - row_max)
        softmax_total = jnp.sum(exp_win, axis=1, keepdims=True) + jnp.sum(
            exp_pil, axis=1, keepdims=True
        )
        prob_win = exp_win / softmax_total
        prob_pil = exp_pil / softmax_total
        weight_win = prob_win.astype(jnp.bfloat16)
        weight_pil = prob_pil.astype(jnp.bfloat16)
        attended = (
            jnp.dot(weight_win, val_head, preferred_element_type=jnp.float32)
            + jnp.dot(weight_pil, pilot_val, preferred_element_type=jnp.float32)
        ).astype(jnp.bfloat16)
        dprob_win = jnp.dot(grad_head, val_head.T, preferred_element_type=jnp.float32)
        dprob_pil = jnp.dot(grad_head, pilot_val.T, preferred_element_type=jnp.float32)
        delta = jnp.sum(
            grad_head.astype(jnp.float32) * attended.astype(jnp.float32), axis=1, keepdims=True
        )
        dscore_win = (prob_win * (dprob_win - delta)).astype(jnp.bfloat16)
        dscore_pil = (prob_pil * (dprob_pil - delta)).astype(jnp.bfloat16)
        query_grad = (
            jnp.dot(dscore_win, key_head, preferred_element_type=jnp.float32)
            + jnp.dot(dscore_pil, pilot_key, preferred_element_type=jnp.float32)
        ) * scaling
        keywin_grad = (
            jnp.dot(dscore_win.T, query_head, preferred_element_type=jnp.float32) * scaling
        )
        valwin_grad = jnp.dot(weight_win.T, grad_head, preferred_element_type=jnp.float32)
        keypil_grad = (
            jnp.dot(dscore_pil.T, query_head, preferred_element_type=jnp.float32) * scaling
        )
        valpil_grad = jnp.dot(weight_pil.T, grad_head, preferred_element_type=jnp.float32)
        return (attended, query_grad, keywin_grad, valwin_grad, keypil_grad, valpil_grad)

    stacked = lax.map(
        one_head,
        (
            split_heads(query_block),
            split_heads(key_win),
            split_heads(val_win),
            split_heads(key_pil),
            split_heads(val_pil),
            split_heads(grad_att),
        ),
    )
    return tuple((join_heads(matrix) for matrix in stacked))


def on_device(
    mapped_askers,
    mapped_lookups,
    mapped_contents,
    result_cotangent,
    result_weight_matrix,
    reference_comb_shift,
    symbol_frame_label,
):
    query_block = mapped_askers[0]
    grad_block = result_cotangent[0]
    overall_line_number = query_block.shape[0]
    model_width = query_block.shape[1]
    group_size = lax.axis_size("seq")
    current_shard_index = lax.axis_index("seq")
    pil_count = reference_comb_shift.shape[1]
    frame_pilots = pil_count * FRAME_SHARDS
    group_bits = FRAME_SHARDS.bit_length() - 1
    gather_bits = list(range(group_bits))
    reduce_bits = list(reversed(gather_bits))
    bit_shape = (2,) + (2,) * group_bits + (pil_count, model_width)
    grad_att = jnp.dot(
        grad_block, result_weight_matrix.T, preferred_element_type=jnp.float32
    ).astype(jnp.bfloat16)
    pair_rows = jnp.stack([mapped_lookups[0], mapped_contents[0]])
    window = with_halo(pair_rows, (("seq", 1),), HALF_SPAN)
    pilot_slots = (
        jnp.arange(pil_count, dtype=jnp.int32) * (overall_line_number // pil_count)
        + reference_comb_shift[0]
    )
    own_pilots = jnp.take(pair_rows, pilot_slots, axis=1)
    frame_pil = own_pilots
    for bit_number in gather_bits:
        partner = swapped(frame_pil, "seq", bit_number)
        upper_side = current_shard_index >> bit_number & 1 == 1
        frame_pil = jnp.where(
            upper_side,
            jnp.concatenate([partner, frame_pil], 1),
            jnp.concatenate([frame_pil, partner], 1),
        )
    held_bits = list(reversed(gather_bits))
    gather_perm = (
        [0]
        + [1 + held_bits.index(bit_number) for bit_number in range(group_bits - 1, -1, -1)]
        + [group_bits + 1, group_bits + 2]
    )
    frame_pil = jnp.transpose(frame_pil.reshape(bit_shape), gather_perm).reshape(
        2, frame_pilots, model_width
    )
    extended_frame_label = jnp.pad(symbol_frame_label, (HALF_SPAN, HALF_SPAN), constant_values=-1)
    neighbor_frame_label = lax.dynamic_slice_in_dim(
        extended_frame_label,
        current_shard_index * overall_line_number,
        overall_line_number + 2 * HALF_SPAN,
        0,
    )
    local_admit_filter = joint_admit_filter(neighbor_frame_label, overall_line_number)
    results = attend_shard(
        query_block, window[0], window[1], frame_pil[0], frame_pil[1], local_admit_filter, grad_att
    )
    attended, query_grad, keywin_grad, valwin_grad, keypil_grad, valpil_grad = results
    mixed_rows = jnp.dot(attended, result_weight_matrix, preferred_element_type=jnp.float32).astype(
        jnp.bfloat16
    )
    weight_share = lax.psum_scatter(
        jnp.dot(attended.T, grad_block, preferred_element_type=jnp.float32),
        ("dp", "seq"),
        scatter_dimension=0,
        tiled=True,
    )
    weight_grad = weight_share / math.sqrt(lax.axis_size("dp") * group_size * overall_line_number)
    win_round = lax.optimization_barrier(jnp.stack([keywin_grad, valwin_grad]).astype(jnp.bfloat16))
    win_grads = win_round.astype(jnp.float32)
    rim_grads = jnp.concatenate(
        [win_round[:, :HALF_SPAN], win_round[:, overall_line_number + HALF_SPAN :]], 1
    )
    beside = with_halo(rim_grads, (("seq", 1),), HALF_SPAN).astype(jnp.float32)
    from_left = beside[:, :HALF_SPAN]
    from_right = beside[:, 3 * HALF_SPAN :]
    pair_grad = win_grads[:, HALF_SPAN : HALF_SPAN + overall_line_number] + from_left + from_right
    pilot_round = lax.optimization_barrier(
        jnp.stack([keypil_grad, valpil_grad]).astype(jnp.bfloat16)
    )
    reduce_perm = (
        [0]
        + [1 + (group_bits - 1 - bit_number) for bit_number in reduce_bits]
        + [group_bits + 1, group_bits + 2]
    )
    pilot_back = jnp.transpose(
        pilot_round.astype(jnp.float32).reshape(bit_shape), reduce_perm
    ).reshape(2, frame_pilots, model_width)
    for bit_number in reduce_bits:
        half_rows = pilot_back.shape[1] // 2
        lower_half = pilot_back[:, :half_rows]
        upper_half = pilot_back[:, half_rows:]
        upper_side = current_shard_index >> bit_number & 1 == 1
        outgoing = jnp.where(upper_side, lower_half, upper_half)
        kept_half = jnp.where(upper_side, upper_half, lower_half)
        pilot_back = kept_half + swapped(outgoing.astype(jnp.bfloat16), "seq", bit_number).astype(
            outgoing.dtype
        )
    pair_grad = pair_grad.at[:, pilot_slots].add(pilot_back)
    return (
        mixed_rows[None],
        query_grad.astype(jnp.bfloat16)[None],
        pair_grad[0].astype(jnp.bfloat16)[None],
        pair_grad[1].astype(jnp.bfloat16)[None],
        weight_grad,
    )


def solution(mesh):
    return jax.shard_map(
        on_device,
        mesh=mesh,
        in_specs=(
            P("dp", "seq", None),
            P("dp", "seq", None),
            P("dp", "seq", None),
            P("dp", "seq", None),
            P(),
            P("seq", None),
            P(),
        ),
        out_specs=(
            P("dp", "seq", None),
            P("dp", "seq", None),
            P("dp", "seq", None),
            P("dp", "seq", None),
            P(("dp", "seq"), None),
        ),
        check_vma=False,
    )
```

profile of v0, /device:TPU:0, one launch (start us, length us, event | category | flops | bytes accessed | tf_op | source)
XLA Modules:
  0.0 479.8 jit_solution(8413420163640871399)
XLA Ops:
  13.4 3.2 pad_maximum_fusion.5
  18.9 3.0 collective-permute-start.2
  21.9 3.6 collective-permute-done.2
  28.9 4.5 collective-permute-start
  34.6 21.4 %collective-permute-done.3 = bf16[2,64,1024]{2,0,1:T(2,128)(2,1)} collective-permute-done((bf16[2,64,1024]{2,0,1:T(2,128)(2,1)S(1)}, bf16[2,64,1024]{2,0,1:T(2,128)(2,1)}, u32[]{:S(2)}, u32[]{:S(2)}) %collective-permute-start.3) | collective-permute-done | bytes 262176 | tf_op jit(solution)/shard_map/ppermute | solution.py:27
  56.1 3.0 broadcast_select_fusion.1
  67.3 3.8 collective-permute-done.4
  71.1 3.5 broadcast_select_fusion
  77.1 3.5 copy.26
  80.6 3.5 copy.24
  84.1 22.8 %pad_maximum_fusion = bf16[2,768,1024]{2,0,1:T(2,128)(2,1)S(1)} fusion(bf16[2,256,1024]{2,0,1:T(2,128)(2,1)} %collective-permute-done.1, bf16[1,256,1024]{2,0,1:T(2,128)(2,1)} %copy-done.5, bf16[1,256,1024]{2,0,1:T(2,128)(2,1)S(1)} %copy.21, bf16[2,256,1024]{2,0,1:T(2,128)(2,1)} %collective-permute-done), kind=kLoop, calls=%fused_computation.87 | loop fusion | flops 12582912 | bytes 6291456 | tf_op jit(solution)/shard_map/concatenate | solution.py:22
  106.8 6.0 %fusion.81 = (bf16[1,768,1024]{2,0,1:T(2,128)(2,1)}, bf16[1,768,1024]{2,0,1:T(2,128)(2,1)}) fusion(bf16[2,768,1024]{2,0,1:T(2,128)(2,1)S(1)} %pad_maximum_fusion), kind=kLoop, calls=%fused_computation.127 | loop fusion | bytes 6291456 | tf_op jit(solution)/shard_map/slice | solution.py:161
  112.8 8.2 %copy.25 = bf16[1,768,1024]{1,2,0:T(8,128)(2,1)} copy(bf16[1,768,1024]{2,0,1:T(2,128)(2,1)} %get-tuple-element.191) | data formatting | bytes 3145728 | tf_op jit(solution)/shard_map/slice | solution.py:161
  121.0 8.2 %copy.23 = bf16[1,768,1024]{1,2,0:T(8,128)(2,1)} copy(bf16[1,768,1024]{2,0,1:T(2,128)(2,1)} %get-tuple-element.192) | data formatting | bytes 3145728 | tf_op jit(solution)/shard_map/slice | solution.py:161
  129.2 160.1 %while.21 = (s32[]{:T(128)}, bf16[8,256,128]{1,2,0:T(8,128)(2,1)}, bf16[8,256,128]{2,1,0:T(8,128)(2,1)}, bf16[8,768,128]{1,2,0:T(8,128)(2,1)}, bf16[8,768,128]{1...) while((s32[]{:T(128)}, bf16[8,256,128]{1,2,0:T(8,128)(2,1)}, ...), condition=%wide.region_6.7_spmd.clone, body=%wide.region_0.6_spmd.clone.sunk | while | flops 408091904 | bytes 14460093 | solution.py:89
  289.3 3.9 fusion.73
  296.2 8.4 %copy.36 = bf16[1,768,1024]{2,0,1:T(2,128)(2,1)} copy(bf16[1,768,1024]{1,2,0:T(8,128)(2,1)} %bitcast.209) | data formatting | bytes 3145728 | tf_op jit(solution)/shard_map/stack;reshape | solution.py:174
  304.7 8.5 %copy.37 = bf16[1,768,1024]{2,0,1:T(2,128)(2,1)} copy(bf16[1,768,1024]{1,2,0:T(8,128)(2,1)} %bitcast.210) | data formatting | bytes 3145728 | tf_op jit(solution)/shard_map/stack;reshape | solution.py:174
  313.1 8.2 %pad_maximum_fusion.1 = bf16[2,768,1024]{2,0,1:T(2,128)(2,1)S(1)} fusion(bf16[1,768,1024]{2,0,1:T(2,128)(2,1)} %copy.37, bf16[1,768,1024]{2,0,1:T(2,128)(2,1)} %copy.36), kind=kLoop, calls=%fused_computation.88 | loop fusion | flops 6291456 | bytes 6291456 | tf_op jit(solution)/shard_map/stack | solution.py:174
  330.0 27.8 %collective-permute-done.8 = bf16[2,64,1024]{1,2,0:T(8,128)(2,1)S(1)} collective-permute-done((bf16[2,64,1024]{1,2,0:T(8,128)(2,1)S(1)}, bf16[2,64,1024]{1,2,0:T(8,128)(2,1)S(1)}, u32[]{:S(2)}, u32[]{:S(2)}) %collective-permute-start.8) | collective-permute-done | bytes 262176 | tf_op jit(solution)/shard_map/ppermute | solution.py:27
  365.4 55.6 %collective-permute-done.9 = bf16[2,32,1024]{1,2,0:T(8,128)(2,1)} collective-permute-done((bf16[2,32,1024]{1,2,0:T(8,128)(2,1)}, bf16[2,32,1024]{1,2,0:T(8,128)(2,1)}, u32[]{:S(2)}, u32[]{:S(2)}) %collective-permute-start.9) | collective-permute-done | bytes 131104 | tf_op jit(solution)/shard_map/ppermute | solution.py:27
  425.0 11.8 %fusion.71 = f32[2,256,1024]{2,0,1:T(2,128)} fusion(bf16[2,256,1024]{2,0,1:T(2,128)(2,1)} %collective-permute-done.6, bf16[2,256,1024]{2,0,1:T(2,128)(2,1)} %get-tuple-element.189, bf16[2,256,1024]{2,0,1:T(2,128)(2,1)} %get-tuple-element.190, bf16[2,256,1024]{2,0,1:T(2,128)(2,1)} %collective-permute-done.5, bf16[2,768,1024]{2,0,1:T(2,128)(2,1)} %copy-done.4), kind=kLoop, calls=%fused_computation.90 | loop fusion | flops 5767168 | bytes 7340032 | tf_op jit(solution)/shard_map/add | solution.py:182
  436.8 4.7 scatter_fusion
  447.3 24.1 %reduce-scatter.2.cloned.1.call-done = f32[32,1024]{1,0:T(8,128)} async-done(((f32[1024,1024]{1,0:T(8,128)}), f32[32,1024]{1,0:T(8,128)}) %reduce-scatter.2.cloned.1.call-update) | async-done | bytes 131088 | tf_op jit(solution)/shard_map/reduce_scatter | solution.py:167
  (264 shorter events, 213.7 us)
Async XLA Ops:
  7.2 53.3 %copy-start = (bf16[1024,1024]{1,0:T(8,128)(2,1)S(1)}, bf16[1024,1024]{1,0:T(8,128)(2,1)}, u32[]{:S(2)}) copy-start(bf16[1024,1024]{1,0:T(8,128)(2,1)} %param.13) | copy-start | bytes 6291460
  7.2 464.2 %reduce-scatter.2.cloned.1.call-start = ((), (), s32[]{:S(2)}) async-start(), calls=%async_computation.1 | async-start | bytes 4325376 | tf_op jit(solution)/shard_map/reduce_scatter | solution.py:167
  18.9 6.6 %collective-permute-start.2 = (bf16[2,32,1024]{2,0,1:T(2,128)(2,1)S(1)}, bf16[2,32,1024]{2,0,1:T(2,128)(2,1)}, u32[]{:S(2)}, u32[]{:S(2)}) collective-permute-start(bf16[2,32,1024]{2,0,1:T(2,128)(2,1)S(1)} %fusion.76), channel_id=1, source_target_pairs={{0,1},{1,0},{2,3},{3,2},{4,5},{5,4},{6,7},{7,6},{8,9},{9,8},{10,11... | collective-permute-start | bytes 393224 | tf_op jit(solution)/shard_map/ppermute | solution.py:27
  27.0 29.0 %collective-permute-start.3 = (bf16[2,64,1024]{2,0,1:T(2,128)(2,1)S(1)}, bf16[2,64,1024]{2,0,1:T(2,128)(2,1)}, u32[]{:S(2)}, u32[]{:S(2)}) collective-permute-start(bf16[2,64,1024]{2,0,1:T(2,128)(2,1)S(1)} %broadcast_select_fusion.2), channel_id=1, source_target_pairs={{0,2},{1,3},{2,0},{3,1},{4,6},{5,7},{6,4},{7,5},{8,10},{9,11},{10,... | collective-permute-start | bytes 786440 | tf_op jit(solution)/shard_map/ppermute | solution.py:27
  28.9 55.2 %collective-permute-start = (bf16[2,256,1024]{2,0,1:T(2,128)(2,1)}, bf16[2,256,1024]{2,0,1:T(2,128)(2,1)}, u32[]{:S(2)}, u32[]{:S(2)}) collective-permute-start(bf16[2,256,1024]{2,0,1:T(2,128)(2,1)} %pad_maximum_fusion.5), channel_id=1, source_target_pairs={{0,1},{1,2},{2,3},{3,4},{4,5},{5,6},{6,7},{7,8},{8,9},{9,10},{10,1... | collective-permute-start | bytes 3145736 | tf_op jit(solution)/shard_map/ppermute | solution.py:20
  33.3 50.7 %collective-permute-start.1 = (bf16[2,256,1024]{2,0,1:T(2,128)(2,1)}, bf16[2,256,1024]{2,0,1:T(2,128)(2,1)}, u32[]{:S(2)}, u32[]{:S(2)}) collective-permute-start(bf16[2,256,1024]{2,0,1:T(2,128)(2,1)} %pad_maximum_fusion.5), channel_id=1, source_target_pairs={{1,0},{2,1},{3,2},{4,3},{5,4},{6,5},{7,6},{8,7},{9,8},{10,9},{11,1... | collective-permute-start | bytes 3145736 | tf_op jit(solution)/shard_map/ppermute | solution.py:21
  34.6 28.5 %copy-start.9 = (s32[4096]{0:T(1024)S(1)}, s32[4096]{0:T(1024)}, u32[]{:S(2)}) copy-start(s32[4096]{0:T(1024)} %param.15) | copy-start | bytes 49156
  59.0 12.1 %collective-permute-start.4 = (bf16[2,128,1024]{2,0,1:T(2,128)(2,1)}, bf16[2,128,1024]{2,0,1:T(2,128)(2,1)}, u32[]{:S(2)}, u32[]{:S(2)}) collective-permute-start(bf16[2,128,1024]{2,0,1:T(2,128)(2,1)} %broadcast_select_fusion.1), channel_id=1, source_target_pairs={{0,4},{1,5},{2,6},{3,7},{4,0},{5,1},{6,2},{7,3},{8,12},{9,13},{10,... | collective-permute-start | bytes 1572872 | tf_op jit(solution)/shard_map/ppermute | solution.py:27
  130.7 5.6 %copy-start.1 = (f32[256,768]{1,0:T(8,128)}, f32[256,768]{1,0:T(8,128)S(1)}, u32[]{:S(2)}) copy-start(f32[256,768]{1,0:T(8,128)S(1)} %get-tuple-element.300) | copy-start | bytes 2359300 | tf_op jit(solution)/shard_map/while
  150.7 5.6 %copy-start.1 = (f32[256,768]{1,0:T(8,128)}, f32[256,768]{1,0:T(8,128)S(1)}, u32[]{:S(2)}) copy-start(f32[256,768]{1,0:T(8,128)S(1)} %get-tuple-element.300) | copy-start | bytes 2359300 | tf_op jit(solution)/shard_map/while
  170.7 5.6 %copy-start.1 = (f32[256,768]{1,0:T(8,128)}, f32[256,768]{1,0:T(8,128)S(1)}, u32[]{:S(2)}) copy-start(f32[256,768]{1,0:T(8,128)S(1)} %get-tuple-element.300) | copy-start | bytes 2359300 | tf_op jit(solution)/shard_map/while
  190.7 5.6 %copy-start.1 = (f32[256,768]{1,0:T(8,128)}, f32[256,768]{1,0:T(8,128)S(1)}, u32[]{:S(2)}) copy-start(f32[256,768]{1,0:T(8,128)S(1)} %get-tuple-element.300) | copy-start | bytes 2359300 | tf_op jit(solution)/shard_map/while
  210.7 5.6 %copy-start.1 = (f32[256,768]{1,0:T(8,128)}, f32[256,768]{1,0:T(8,128)S(1)}, u32[]{:S(2)}) copy-start(f32[256,768]{1,0:T(8,128)S(1)} %get-tuple-element.300) | copy-start | bytes 2359300 | tf_op jit(solution)/shard_map/while
  230.7 5.6 %copy-start.1 = (f32[256,768]{1,0:T(8,128)}, f32[256,768]{1,0:T(8,128)S(1)}, u32[]{:S(2)}) copy-start(f32[256,768]{1,0:T(8,128)S(1)} %get-tuple-element.300) | copy-start | bytes 2359300 | tf_op jit(solution)/shard_map/while
  250.7 5.6 %copy-start.1 = (f32[256,768]{1,0:T(8,128)}, f32[256,768]{1,0:T(8,128)S(1)}, u32[]{:S(2)}) copy-start(f32[256,768]{1,0:T(8,128)S(1)} %get-tuple-element.300) | copy-start | bytes 2359300 | tf_op jit(solution)/shard_map/while
  270.8 5.6 %copy-start.1 = (f32[256,768]{1,0:T(8,128)}, f32[256,768]{1,0:T(8,128)S(1)}, u32[]{:S(2)}) copy-start(f32[256,768]{1,0:T(8,128)S(1)} %get-tuple-element.300) | copy-start | bytes 2359300 | tf_op jit(solution)/shard_map/while
  296.2 25.2 %collective-permute-start.7 = (bf16[2,128,1024]{1,2,0:T(8,128)(2,1)S(1)}, bf16[2,128,1024]{1,2,0:T(8,128)(2,1)S(1)}, u32[]{:S(2)}, u32[]{:S(2)}) collective-permute-start(bf16[2,128,1024]{1,2,0:T(8,128)(2,1)S(1)} %select_convert_fusion.2), channel_id=1, source_target_pairs={{0,4},{1,5},{2,6},{3,7},{4,0},{5,1},{6,2},{7,3},{8,12},{9,13},{10,... | collective-permute-start | bytes 1572872 | tf_op jit(solution)/shard_map/ppermute | solution.py:27
  313.1 8.2 %copy-start.3 = (f32[2,256,1024]{1,2,0:T(8,128)S(1)}, f32[2,256,1024]{1,2,0:T(8,128)}, u32[]{:S(2)}) copy-start(f32[2,256,1024]{1,2,0:T(8,128)} %copy-done.2) | copy-start | bytes 6291460
  321.3 2.7 copy-start.4
  321.7 36.1 %collective-permute-start.8 = (bf16[2,64,1024]{1,2,0:T(8,128)(2,1)S(1)}, bf16[2,64,1024]{1,2,0:T(8,128)(2,1)S(1)}, u32[]{:S(2)}, u32[]{:S(2)}) collective-permute-start(bf16[2,64,1024]{1,2,0:T(8,128)(2,1)S(1)} %select_convert_fusion.1), channel_id=1, source_target_pairs={{0,2},{1,3},{2,0},{3,1},{4,6},{5,7},{6,4},{7,5},{8,10},{9,11},{10,... | collective-permute-start | bytes 786440 | tf_op jit(solution)/shard_map/ppermute | solution.py:27
  326.5 98.5 %collective-permute-start.5 = (bf16[2,256,1024]{2,0,1:T(2,128)(2,1)}, bf16[2,256,1024]{2,0,1:T(2,128)(2,1)}, u32[]{:S(2)}, u32[]{:S(2)}) collective-permute-start(bf16[2,256,1024]{2,0,1:T(2,128)(2,1)} %get-tuple-element.189), channel_id=1, source_target_pairs={{0,1},{1,2},{2,3},{3,4},{4,5},{5,6},{6,7},{7,8},{8,9},{9,10},{10,1... | collective-permute-start | bytes 3145736 | tf_op jit(solution)/shard_map/ppermute | solution.py:20
  328.7 96.3 %collective-permute-start.6 = (bf16[2,256,1024]{2,0,1:T(2,128)(2,1)}, bf16[2,256,1024]{2,0,1:T(2,128)(2,1)}, u32[]{:S(2)}, u32[]{:S(2)}) collective-permute-start(bf16[2,256,1024]{2,0,1:T(2,128)(2,1)} %get-tuple-element.190), channel_id=1, source_target_pairs={{1,0},{2,1},{3,2},{4,3},{5,4},{6,5},{7,6},{8,7},{9,8},{10,9},{11,1... | collective-permute-start | bytes 3145736 | tf_op jit(solution)/shard_map/ppermute | solution.py:21
  358.2 4.1 copy-start.6
  359.2 61.8 %collective-permute-start.9 = (bf16[2,32,1024]{1,2,0:T(8,128)(2,1)}, bf16[2,32,1024]{1,2,0:T(8,128)(2,1)}, u32[]{:S(2)}, u32[]{:S(2)}) collective-permute-start(bf16[2,32,1024]{1,2,0:T(8,128)(2,1)} %select_convert_fusion), channel_id=1, source_target_pairs={{0,1},{1,0},{2,3},{3,2},{4,5},{5,4},{6,7},{7,6},{8,9},{9,8},{10,11... | collective-permute-start | bytes 393224 | tf_op jit(solution)/shard_map/ppermute | solution.py:27
  (4 other events, 4.6 us)
Sparse Core Ops, SparseCore 0:
  293.4 177.9 reduce-scatter.1
where the time goes:
time: 486 us; the launch traced here: 480 us
  matrix products  145 us (30%)
  waiting for transfers between devices  136 us (28%)
  local copies, waits for them, and re-layouts  85.6 us (18%)
  other arithmetic  79.1 us (16%)
  starting transfers between devices  18.4 us (4%)
  between operations  14.3 us (3%)
    ppermute x6, waiting for transfers between devices, swapped(): lax.ppermute(value, axis, [(i, i ^ 1 << apart) for i in range(lax.axis_si...  112 us
    reduce_scatter x1, waiting for transfers between devices, on_device(): lax.psum_scatter(jnp.dot(attended.T, grad_block, preferred_element_type=j...  24.1 us
    concatenate x1, other arithmetic, with_halo(): value = jnp.concatenate([before, value, after], axis=dim)  22.8 us
    dot_general x8, matrix products, one_head(): jnp.dot(weight_win.T, grad_head, preferred_element_type=jnp.float32)  17.8 us
    another operation x2, local copies, waits for them, and re-layouts, on_device(): jnp.stack([keywin_grad, valwin_grad]).astype(jnp.bfloat16)  16.9 us
    dot_general x8, matrix products, one_head(): jnp.dot(weight_win, val_head, preferred_element_type=jnp.float32)  15.8 us
    dot_general x8, matrix products, one_head(): jnp.dot(dscore_win, key_head, preferred_element_type=jnp.float32)  14.6 us
    slice x2, local copies, waits for them, and re-layouts, on_device(): window[1]  14.2 us
  transfers between devices with their start and end apart: 11, of which 6 were waited for; matrix products, arithmetic and copies ran while one was open for 18% of the time, Pallas kernels for 0%

commit v1 on v0

v1 whole, which is shorter than its diff:
```python
import functools
import math

import jax
import jax.numpy as jnp
from jax import lax
from jax.experimental import pallas as pl
from jax.experimental.pallas import tpu as pltpu
from jax.sharding import PartitionSpec as P

HEADS = 8
HALF_SPAN = 256
FRAME_SHARDS = 8
MESH = pl.DeviceIdType.MESH
F32 = jnp.float32
BF16 = jnp.bfloat16


def dot_nt(a, b):
    return lax.dot_general(a, b, (((1,), (1,)), ((), ())), preferred_element_type=F32)


def dot_tn(a, b):
    return lax.dot_general(a, b, (((0,), (0,)), ((), ())), preferred_element_type=F32)


def dot_nn(a, b):
    return lax.dot_general(a, b, (((1,), (0,)), ((), ())), preferred_element_type=F32)


def attention_kernel(
    frames,
    rows,
    head_dim,
    pil,
    k_ref,
    v_ref,
    q_ref,
    g_ref,
    p_ref,
    klab_ref,
    qlab_ref,
    att_ref,
    dq_ref,
    dk_ref,
    dv_ref,
    kb,
    vb,
    qb,
    gb,
    pb,
    kpil,
    vpil,
    dka,
    dva,
    dkp,
    dvp,
    att_st,
    dq_st,
    dk_st,
    dv_st,
    hg_out,
    hg_in,
    send_in,
    recv_in,
    loc_in,
    send_h,
    recv_h,
    send_hg,
    recv_hg,
    send_out,
    recv_out,
    loc_out,
):
    seq = lax.axis_index("seq")
    me = seq % FRAME_SHARDS
    frame = seq // FRAME_SHARDS
    base = frame * FRAME_SHARDS
    has_left = frame > 0
    has_right = frame < frames - 1
    scale = 1.0 / math.sqrt(head_dim)
    n = FRAME_SHARDS

    def cols(h):
        return pl.ds(pl.multiple_of(h * head_dim, head_dim), head_dim)

    def block(b):
        return pl.ds(pl.multiple_of(b * rows, rows), rows)

    barrier = pltpu.get_barrier_semaphore()

    def greet(t, carry):
        pl.semaphore_signal(
            barrier, inc=1, device_id={"seq": base + (me + t) % n}, device_id_type=MESH
        )
        return carry

    lax.fori_loop(1, n, greet, 0)

    @pl.when(has_left)
    def _():
        pl.semaphore_signal(barrier, inc=1, device_id={"seq": seq - n}, device_id_type=MESH)

    @pl.when(has_right)
    def _():
        pl.semaphore_signal(barrier, inc=1, device_id={"seq": seq + n}, device_id_type=MESH)

    sides = has_left.astype(jnp.int32) + has_right.astype(jnp.int32)
    pl.semaphore_wait(barrier, n - 1 + sides)

    def source(i, peer):
        if i == 0:
            return p_ref
        return (k_ref, v_ref, q_ref, g_ref)[i - 1].at[:, cols(peer)]

    def landing(i, src):
        if i == 0:
            return pb.at[src]
        if i <= 2:
            return (kb, vb)[i - 1].at[block(src + 1)]
        return (qb, gb)[i - 3].at[block(src)]

    def in_copy(i, peer, src):
        return pltpu.make_async_remote_copy(
            src_ref=source(i, peer),
            dst_ref=landing(i, src),
            send_sem=send_in.at[i, peer],
            recv_sem=recv_in.at[i, src],
            device_id={"seq": base + peer},
            device_id_type=MESH,
        )

    for i in range(5):

        def send_one(t, carry, i=i):
            in_copy(i, (me + t) % n, me).start()
            return carry

        lax.fori_loop(1, n, send_one, 0)
        pltpu.make_async_copy(source(i, me), landing(i, me), loc_in.at[i]).start()

    zero_halo = jnp.zeros((rows, head_dim), BF16)

    @pl.when(jnp.logical_not(has_left))
    def _():
        kb[0:rows] = zero_halo
        vb[0:rows] = zero_halo

    @pl.when(jnp.logical_not(has_right))
    def _():
        kb[(n + 1) * rows : (n + 2) * rows] = zero_halo
        vb[(n + 1) * rows : (n + 2) * rows] = zero_halo

    dka[...] = jnp.zeros_like(dka)
    dva[...] = jnp.zeros_like(dva)
    dkp[...] = jnp.zeros_like(dkp)
    dvp[...] = jnp.zeros_like(dvp)

    def wait_in(i):
        def wait_one(t, carry):
            in_copy(i, (me + t) % n, (me + t) % n).wait_recv()
            return carry

        lax.fori_loop(1, n, wait_one, 0)
        pltpu.make_async_copy(source(i, me), landing(i, me), loc_in.at[i]).wait()

    def halo_copy(i, to_right):
        buf = (kb, vb)[i]
        s = 2 * i + (0 if to_right else 1)
        return pltpu.make_async_remote_copy(
            src_ref=buf.at[pl.ds((n if to_right else 1) * rows, rows)],
            dst_ref=buf.at[pl.ds((0 if to_right else n + 1) * rows, rows)],
            send_sem=send_h.at[s],
            recv_sem=recv_h.at[s],
            device_id={"seq": seq + n if to_right else seq - n},
            device_id_type=MESH,
        )

    wait_in(0)
    for i in range(2):
        wait_in(1 + i)

        @pl.when(has_right)
        def _(i=i):
            halo_copy(i, True).start()

        @pl.when(has_left)
        def _(i=i):
            halo_copy(i, False).start()

        def pick(s, carry, i=i):
            picked = dot_nn(pb[s], (kb, vb)[i][block(s + 1), :])
            (kpil, vpil)[i][s] = picked.astype(BF16)
            return carry

        lax.fori_loop(0, n, pick, 0)
    wait_in(3)
    wait_in(4)

    for i in range(2):

        @pl.when(has_right)
        def _(i=i):
            halo_copy(i, True).wait_send()
            halo_copy(i, False).wait_recv()

        @pl.when(has_left)
        def _(i=i):
            halo_copy(i, False).wait_send()
            halo_copy(i, True).wait_recv()

    stages = (att_st, dq_st, dk_st, dv_st)
    outs = (att_ref, dq_ref, dk_ref, dv_ref)

    def out_copy(i, peer, col):
        return pltpu.make_async_remote_copy(
            src_ref=stages[i].at[peer],
            dst_ref=outs[i].at[:, cols(col)],
            send_sem=send_out.at[i, peer],
            recv_sem=recv_out.at[i, col],
            device_id={"seq": base + peer},
            device_id_type=MESH,
        )

    def own_copy(i):
        return pltpu.make_async_copy(stages[i].at[me], outs[i].at[:, cols(me)], loc_out.at[i])

    def ship(i, b):
        @pl.when(b != me)
        def _():
            out_copy(i, b, me).start()

        @pl.when(b == me)
        def _():
            own_copy(i).start()

    span = rows + 2 * HALF_SPAN
    key_at = lax.broadcasted_iota(jnp.int32, (span, rows), 0)
    query_at = lax.broadcasted_iota(jnp.int32, (span, rows), 1)
    near = (key_at >= query_at) & (key_at <= query_at + 2 * HALF_SPAN)
    to_exp2 = scale * math.log2(math.e)

    def query_block(t, carry):
        b = (me + 1 + t) % n
        wide = pl.ds(pl.multiple_of(b * rows, rows), span)
        q = qb[block(b), :]
        g = gb[block(b), :]
        kw = kb[wide, :]
        vw = vb[wide, :]
        kp = kpil[...].reshape(n * pil, head_dim)
        vp = vpil[...].reshape(n * pil, head_dim)
        mask = near & (klab_ref[wide, :] == qlab_ref[pl.ds(b, 1), :])
        s_w = jnp.where(mask, dot_nt(kw, q), -jnp.inf)
        s_p = dot_nt(kp, q)
        top = jnp.maximum(jnp.max(s_w, 0, keepdims=True), jnp.max(s_p, 0, keepdims=True))
        e_w = jnp.exp2((s_w - top) * to_exp2)
        e_p = jnp.exp2((s_p - top) * to_exp2)
        inv = 1.0 / (jnp.sum(e_w, 0, keepdims=True) + jnp.sum(e_p, 0, keepdims=True))
        p_w = e_w * inv
        p_p = e_p * inv
        w_w = p_w.astype(BF16)
        w_p = p_p.astype(BF16)
        att_t = (dot_tn(vw, w_w) + dot_tn(vp, w_p)).astype(BF16).astype(F32)
        att_st[b] = att_t.T.astype(BF16)
        ship(0, b)
        delta = jnp.sum(g.astype(F32).T * att_t, 0, keepdims=True)
        d_w = (p_w * (dot_nt(vw, g) - delta)).astype(BF16)
        d_p = (p_p * (dot_nt(vp, g) - delta)).astype(BF16)
        dq_t = (dot_tn(kw, d_w) + dot_tn(kp, d_p)) * scale
        dq_st[b] = dq_t.T.astype(BF16)
        ship(1, b)
        dva[wide, :] += dot_nn(w_w, g)
        dvp[...] += dot_nn(w_p, g)
        dka[wide, :] += dot_nn(d_w, q)
        dkp[...] += dot_nn(d_p, q)
        return carry

    lax.fori_loop(0, n, query_block, 0)

    def edge_copy(i, to_right):
        s = 2 * i + (0 if to_right else 1)
        return pltpu.make_async_remote_copy(
            src_ref=hg_out.at[s],
            dst_ref=hg_in.at[s],
            send_sem=send_hg.at[s],
            recv_sem=recv_hg.at[s],
            device_id={"seq": seq + n if to_right else seq - n},
            device_id_type=MESH,
        )

    factor = (scale, 1.0)
    sums = (dka, dva)
    pilot_sums = (dkp, dvp)
    for i in range(2):

        @pl.when(has_right)
        def _(i=i):
            hg_out[2 * i] = (sums[i][(n + 1) * rows : (n + 2) * rows, :] * factor[i]).astype(BF16)
            edge_copy(i, True).start()

        @pl.when(has_left)
        def _(i=i):
            hg_out[2 * i + 1] = (sums[i][0:rows, :] * factor[i]).astype(BF16)
            edge_copy(i, False).start()

    def finish(i, s):
        pilots = pilot_sums[i][pl.ds(pl.multiple_of(s * pil, pil), pil), :]
        high = pilots.astype(BF16)
        low = (pilots - high.astype(F32)).astype(BF16)
        places = pb[s]
        total = sums[i][block(s + 1), :] + (dot_tn(places, high) + dot_tn(places, low))
        return total * factor[i]

    def middle(t, carry):
        s = (me + 1 + t) % n

        @pl.when((s != 0) & (s != n - 1))
        def _():
            for i in range(2):
                stages[2 + i][s] = finish(i, s).astype(BF16)
                ship(2 + i, s)

        return carry

    lax.fori_loop(0, n, middle, 0)
    for i in range(2):

        @pl.when(has_left)
        def _(i=i):
            edge_copy(i, False).wait_send()
            edge_copy(i, True).wait_recv()
            stages[2 + i][0] = (finish(i, 0) + hg_in[2 * i].astype(F32)).astype(BF16)

        @pl.when(jnp.logical_not(has_left))
        def _(i=i):
            stages[2 + i][0] = finish(i, 0).astype(BF16)

        ship(2 + i, 0)

        @pl.when(has_right)
        def _(i=i):
            edge_copy(i, True).wait_send()
            edge_copy(i, False).wait_recv()
            stages[2 + i][n - 1] = (finish(i, n - 1) + hg_in[2 * i + 1].astype(F32)).astype(BF16)

        @pl.when(jnp.logical_not(has_right))
        def _(i=i):
            stages[2 + i][n - 1] = finish(i, n - 1).astype(BF16)

        ship(2 + i, n - 1)

    def drain(t, carry):
        peer = (me + t) % n
        for i in range(5):
            in_copy(i, peer, me).wait_send()
        for i in range(4):
            out_copy(i, peer, me).wait_send()
            out_copy(i, peer, peer).wait_recv()
        return carry

    lax.fori_loop(1, n, drain, 0)
    for i in range(4):
        own_copy(i).wait()


def attend(k, v, q, g, places, key_labels, query_labels, frames):
    rows, width = q.shape
    head_dim = width // HEADS
    pil = places.shape[0]
    n = FRAME_SHARDS
    out = jax.ShapeDtypeStruct((rows, width), BF16)
    hbm = pl.BlockSpec(memory_space=pl.ANY)
    vmem = pl.BlockSpec(memory_space=pltpu.VMEM)
    dma = pltpu.SemaphoreType.DMA
    return pl.pallas_call(
        functools.partial(attention_kernel, frames, rows, head_dim, pil),
        out_shape=(out,) * 4,
        in_specs=[hbm] * 5 + [vmem] * 2,
        out_specs=(hbm,) * 4,
        scratch_shapes=[
            pltpu.VMEM(((n + 2) * rows, head_dim), BF16),
            pltpu.VMEM(((n + 2) * rows, head_dim), BF16),
            pltpu.VMEM((n * rows, head_dim), BF16),
            pltpu.VMEM((n * rows, head_dim), BF16),
            pltpu.VMEM((n, pil, rows), BF16),
            pltpu.VMEM((n, pil, head_dim), BF16),
            pltpu.VMEM((n, pil, head_dim), BF16),
            pltpu.VMEM(((n + 2) * rows, head_dim), F32),
            pltpu.VMEM(((n + 2) * rows, head_dim), F32),
            pltpu.VMEM((n * pil, head_dim), F32),
            pltpu.VMEM((n * pil, head_dim), F32),
            pltpu.VMEM((n, rows, head_dim), BF16),
            pltpu.VMEM((n, rows, head_dim), BF16),
            pltpu.VMEM((n, rows, head_dim), BF16),
            pltpu.VMEM((n, rows, head_dim), BF16),
            pltpu.VMEM((4, rows, head_dim), BF16),
            pltpu.VMEM((4, rows, head_dim), BF16),
            dma((5, n)),
            dma((5, n)),
            dma((5,)),
            dma((4,)),
            dma((4,)),
            dma((4,)),
            dma((4,)),
            dma((4, n)),
            dma((4, n)),
            dma((4,)),
        ],
        compiler_params=pltpu.CompilerParams(
            collective_id=0, has_side_effects=True, vmem_limit_bytes=40 * 1024 * 1024
        ),
    )(k, v, q, g, places, key_labels, query_labels)


def on_device(
    mapped_askers,
    mapped_lookups,
    mapped_contents,
    result_cotangent,
    result_weight_matrix,
    reference_comb_shift,
    symbol_frame_label,
):
    grad_block = result_cotangent[0]
    rows = grad_block.shape[0]
    shards = lax.axis_size("seq")
    frames = shards // FRAME_SHARDS
    pil = reference_comb_shift.shape[1]
    frame = lax.axis_index("seq") // FRAME_SHARDS
    grad_att = jnp.dot(grad_block, result_weight_matrix.T, preferred_element_type=F32).astype(BF16)
    slots = jnp.arange(pil, dtype=jnp.int32) * (rows // pil) + reference_comb_shift[0]
    places = (slots[:, None] == jnp.arange(rows, dtype=jnp.int32)[None, :]).astype(BF16)
    extended = jnp.pad(symbol_frame_label, (HALF_SPAN, HALF_SPAN), constant_values=-1)
    tokens = FRAME_SHARDS * rows
    key_labels = lax.dynamic_slice_in_dim(extended, frame * tokens, tokens + 2 * HALF_SPAN, 0)
    query_labels = key_labels[HALF_SPAN : HALF_SPAN + tokens].reshape(FRAME_SHARDS, rows)
    attended, query_grad, key_grad, value_grad = attend(
        mapped_lookups[0],
        mapped_contents[0],
        mapped_askers[0],
        grad_att,
        places,
        key_labels[:, None],
        query_labels,
        frames,
    )
    mixed = jnp.dot(attended, result_weight_matrix, preferred_element_type=F32).astype(BF16)
    share = lax.dot_general(
        attended, grad_block, (((0,), (0,)), ((), ())), preferred_element_type=F32
    )
    total = lax.psum_scatter(share, ("dp", "seq"), scatter_dimension=0, tiled=True)
    weight_grad = total / math.sqrt(lax.axis_size("dp") * shards * rows)
    return (mixed[None], query_grad[None], key_grad[None], value_grad[None], weight_grad)


def solution(mesh):
    row_spec = P("dp", "seq", None)
    return jax.shard_map(
        on_device,
        mesh=mesh,
        in_specs=(row_spec, row_spec, row_spec, row_spec, P(), P("seq", None), P()),
        out_specs=(row_spec, row_spec, row_spec, row_spec, P(("dp", "seq"), None)),
        check_vma=False,
    )
```

time: 486 us -> 245 us (0.50); the launches traced: 480 us -> 245 us
  matrix products: 145 us -> 5.98 us
  other arithmetic: 79.1 us -> 2.43 us
  local copies, waits for them, and re-layouts: 85.6 us -> 10.9 us
  Pallas kernels: 0 us -> 69.3 us
  starting transfers between devices: 18.4 us -> 0.04 us
  waiting for transfers between devices: 136 us -> 142 us
    dot_general x99 -> x3, matrix products: 145 us -> 5.98 us  [the longest x1 2.7 us: on_device(): lax.dot_general(attended, grad_block, (((0,), (0,)), ((), ())), preferred...]
    reduce_scatter x1, waiting for transfers between devices: 24.1 us -> 142 us  [on_device(): lax.psum_scatter(share, ('dp', 'seq'), scatter_dimension=0, tiled=True)]
    ppermute x10 -> x0, waiting for transfers between devices: 112 us -> none  [the longest x6 112 us: swapped(): lax.ppermute(value, axis, [(i, i ^ 1 << apart) for i in range(lax.axis_si...]
    pallas_call x0 -> x1, Pallas kernels: none -> 69.3 us  [attend(): pl.pallas_call(functools.partial(attention_kernel, frames, rows, head_dim...]
    slice x9 -> x2, local copies, waits for them, and re-layouts: 35.8 us -> 0.81 us  [on_device(): key_labels[HALF_SPAN:HALF_SPAN + tokens].reshape(FRAME_SHARDS, rows)]
    concatenate x1 -> x0, other arithmetic: 22.8 us -> none  [with_halo(): value = jnp.concatenate([before, value, after], axis=dim)]
    ppermute x10 -> x0, starting transfers between devices: 18.4 us -> none  [the longest x6 9.08 us: swapped(): lax.ppermute(value, axis, [(i, i ^ 1 << apart) for i in range(lax.axis_si...]
    another operation x2 -> x0, local copies, waits for them, and re-layouts: 16.9 us -> none  [on_device(): jnp.stack([keywin_grad, valwin_grad]).astype(jnp.bfloat16)]
  transfers between devices with their start and end apart: 11 -> 1, of which waited for: 6 -> 1; matrix products, arithmetic and copies ran while one was open for 18% -> 1% of each run, Pallas kernels for 0% -> 0%
where the time goes in v1:
time: 245 us
  waiting for transfers between devices  142 us (58%)
  Pallas kernels  69.3 us (28%)
  between operations  14.1 us (6%)
  local copies, waits for them, and re-layouts  10.9 us (4%)
  matrix products  5.98 us (2%)
    reduce_scatter x1, waiting for transfers between devices, on_device(): lax.psum_scatter(share, ('dp', 'seq'), scatter_dimension=0, tiled=True)  142 us
    pallas_call x1, Pallas kernels, attend(): pl.pallas_call(functools.partial(attention_kernel, frames, rows, head_dim...  69.3 us
    unnamed x25, local copies, waits for them, and re-layouts  8.74 us
  transfers between devices with their start and end apart: 1, of which 1 were waited for; matrix products, arithmetic and copies ran while one was open for 1% of the time, Pallas kernels for 0%

profile of v1, /device:TPU:0, one launch (start us, length us, event | category | flops | bytes accessed | tf_op | source)
XLA Modules:
  0.0 244.6 jit_solution(9201290694047681456)
XLA Ops:
  7.2 0.0 copy-start
  7.2 0.0 reduce-scatter.2.cloned.1.call-start
  7.2 0.9 pad_dynamic-slice_fusion.1
  8.2 0.4 broadcast_in_dim.22.klab_ref
  8.6 0.8 pad_dynamic-slice_fusion
  9.4 0.0 copy-start.9
  9.4 0.8 bitcast_add_fusion
  10.2 0.1 fusion.4.p_ref
  10.3 1.8 convolution_convert_fusion.1.g_ref
  12.1 0.0 copy-start.10
  12.1 69.3 %shard_map.110 = (bf16[256,1024]{1,0:T(8,128)(2,1)S(1)}, bf16[256,1024]{1,0:T(8,128)(2,1)S(1)}, bf16[256,1024]{1,0:T(8,128)(2,1)S(1)}, bf16[256,1024]{1,0:T(8,128)(2,1)S(1)}) custom-call(bf16[256,1024]{1,0:T(8,128)(2,1)S(1)} %bitcast.22, bf16[256,1024]{1,0:T(8,128)(2,1)S(1)} %bitcast.23, bf16[256,1024]{1,0:T(8,128)(2,1)S(1)} %bitcast.24, ...), custom_call_target="tpu_custom_call" | custom-call | tf_op jit(solution)/shard_map/pallas_call | solution.py:375
  81.4 0.8 copy-done.3
  82.2 0.8 copy-done.5
  83.0 0.8 copy-done.6
  83.8 0.8 copy-done.1
  84.6 2.7 %fusion.1 = f32[1024,1024]{1,0:T(8,128)} fusion(bf16[256,1024]{1,0:T(8,128)(2,1)S(1)} %get-tuple-element.9, bf16[1,256,1024]{2,1,0:T(8,128)(2,1)S(1)} %copy-done.10), kind=kOutput, calls=%fused_computation.3 | convolution fusion | flops 536870912 | bytes 5242880 | tf_op jit(solution)/shard_map/dot_general | solution.py:448
  87.3 0.0 reduce-scatter.2.cloned.1.call-update
  87.3 1.0 copy-done.2
  88.3 1.5 fusion
  89.8 141.8 %reduce-scatter.2.cloned.1.call-done = f32[32,1024]{1,0:T(8,128)} async-done(((f32[1024,1024]{1,0:T(8,128)}), f32[32,1024]{1,0:T(8,128)}) %reduce-scatter.2.cloned.1.call-update) | async-done | bytes 131088 | tf_op jit(solution)/shard_map/reduce_scatter | solution.py:451
  231.6 1.6 broadcast_multiply_fusion
  233.2 1.9 copy.16
  235.1 1.9 copy.17
  237.0 0.8 copy.18
  (15 shorter events, 0.0 us)
Async XLA Ops:
  7.2 3.1 %copy-start = (bf16[1024,1024]{1,0:T(8,128)(2,1)S(1)}, bf16[1024,1024]{1,0:T(8,128)(2,1)}, u32[]{:S(2)}) copy-start(bf16[1024,1024]{1,0:T(8,128)(2,1)} %param.11) | copy-start | bytes 6291460
  7.2 224.5 %reduce-scatter.2.cloned.1.call-start = ((), (), s32[]{:S(2)}) async-start(), calls=%async_computation.1 | async-start | bytes 4325376 | tf_op jit(solution)/shard_map/reduce_scatter | solution.py:451
  9.4 2.7 %copy-start.7 = (bf16[1,256,1024]{2,1,0:T(8,128)(2,1)S(1)}, bf16[1,256,1024]{2,1,0:T(8,128)(2,1)}, u32[]{:S(2)}) copy-start(bf16[1,256,1024]{2,1,0:T(8,128)(2,1)} %param.8) | copy-start | bytes 1572868
  9.4 2.7 %copy-start.8 = (bf16[1,256,1024]{2,1,0:T(8,128)(2,1)S(1)}, bf16[1,256,1024]{2,1,0:T(8,128)(2,1)}, u32[]{:S(2)}) copy-start(bf16[1,256,1024]{2,1,0:T(8,128)(2,1)} %param.9) | copy-start | bytes 1572868
  9.4 2.7 %copy-start.9 = (bf16[1,256,1024]{2,1,0:T(8,128)(2,1)S(1)}, bf16[1,256,1024]{2,1,0:T(8,128)(2,1)}, u32[]{:S(2)}) copy-start(bf16[1,256,1024]{2,1,0:T(8,128)(2,1)} %param.7) | copy-start | bytes 1572868
  12.1 72.5 %copy-start.10 = (bf16[1,256,1024]{2,1,0:T(8,128)(2,1)S(1)}, bf16[1,256,1024]{2,1,0:T(8,128)(2,1)}, u32[]{:S(2)}) copy-start(bf16[1,256,1024]{2,1,0:T(8,128)(2,1)} %param.10) | copy-start | bytes 1572868
  81.4 0.8 copy-start.3
  82.2 0.8 copy-start.5
  83.0 0.8 copy-start.6
  83.8 0.8 copy-start.1
  87.3 1.0 copy-start.2
  88.3 148.6 %copy-start.4 = (bf16[256,1024]{1,0:T(8,128)(2,1)S(1)}, bf16[256,1024]{1,0:T(8,128)(2,1)}, u32[]{:S(2)}) copy-start(bf16[256,1024]{1,0:T(8,128)(2,1)} %copy-done.3) | copy-start | bytes 1572868
Sparse Core Ops, SparseCore 0:
  87.4 144.1 reduce-scatter.1
